TPU v7x, 32 devices: a whole 2x2x4 slice. The times are simulated.
32 devices in a mesh: gx: 8 (over z, core), gy: 4 (over y, x).
Axes of the slice: x: 2, y: 2, z: 4, core: 2. Of those that a mesh axis runs over, the one named last changes fastest.
Arguments:
- pressure0: float32 [4, 128, 512], P(None, 'gx', 'gy'), may hold values from -6 to 6
- saturation0: float32 [4, 128, 512], P(None, 'gx', 'gy'), may hold values from 0.1 to 0.9
- trans_x: float32 [4, 128, 512], P(None, 'gx', 'gy'), may hold values from 0.1 to 2
- trans_y: float32 [4, 128, 512], P(None, 'gx', 'gy'), may hold values from 0.1 to 2
- trans_z: float32 [3, 128, 512], P(None, 'gx', 'gy'), may hold values from 0.05 to 1
- pore_volume: float32 [4, 128, 512], P(None, 'gx', 'gy'), may hold values from 0.5 to 2
- upwind: int32 [4, 128, 512], P(None, 'gx', 'gy'), may hold values from 0 to 63
- well_cell: int32 [8, 4, 64], P('gx', 'gy'), may hold values from 0 to 8191
- well_rate: float32 [8, 4, 64], P('gx', 'gy'), may hold values from -8 to 8
- plan: int32 [2, 8, 4, 64], P(None, 'gx', 'gy'), may hold values from 0 to 2
- observed: float32 [2, 2, 8, 4, 64], P(None, None, 'gx', 'gy'), may hold values from -6 to 6
Outputs:
- grad_x: float32 [4, 128, 512], P(None, 'gx', 'gy')
- grad_y: float32 [4, 128, 512], P(None, 'gx', 'gy')
- grad_z: float32 [3, 128, 512], P(None, 'gx', 'gy')
Inputs may be any that keep to these rules, and one draw needn't show every extreme that they name: `upwind`: bit 3 n + d of an entry is 1 where the cell itself is upstream of its forward face along x, y or layers (d = 0, 1, 2) in step n, 0 where the next cell is. `well_cell`: a cell of the well's own tile, numbered layer by layer, then row, then column. `plan`: 0 shut, 1 half rate, 2 full rate.
All inputs are finite; a program needn't handle non-finite values.
Results may differ from a plain program's by a relative error of at most 0.0001.
Values sent between devices are 32-bit elements; how exact they have to be, the bound alone decides.
No kernel may reach another device: no remote copies, remote signals or barrier semaphores. Data moves between devices by JAX's collectives and lax.ppermute only.
A program may use at most 64 MiB of HBM per device.

v0:
```python
import jax
import jax.numpy as jnp
from jax import lax
from jax.experimental import pallas as pl
from jax.experimental.pallas import tpu as pltpu
from jax.sharding import PartitionSpec as P

time_step = 0.05

GROUPS = {"p": (0, 4), "s": (4, 4), "tx": (8, 4), "ty": (12, 4), "tz": (16, 3), "pv": (19, 4), "up": (23, 4)}
ORDER = ("p", "s", "tx", "ty", "tz", "pv", "up")
COUNT = 27
SLOT = 10
SLOTS = 12
PIECES = COUNT * 4 + 4
PACKED = -(-PIECES // SLOTS)


FIELDS = 11


def pack_rows(*refs):
    p, s, tx, ty, tz, pv, up, cell, rate, plan, observed = refs[:FIELDS]
    own, far, near, upi, cells, rates, plans, seen, sems = refs[FIELDS:]
    targets = [own.at[pl.ds(*GROUPS[name])] for name in ORDER[:6]] + [upi, cells, rates, plans, seen]
    copies = [
        pltpu.make_async_copy(source, target, sems.at[k])
        for k, (source, target) in enumerate(zip(refs[:FIELDS], targets))
    ]
    for copy in copies:
        copy.start()
    for copy in copies:
        copy.wait()
    first = GROUPS["up"][0]
    for layer in range(4):
        own[first + layer] = upi[layer].astype(jnp.float32)
    own[COUNT] = jnp.zeros((16, 128), jnp.float32)
    own[COUNT, 0:1, 0:64] = cells[0].astype(jnp.float32)
    own[COUNT, 1:2, 0:64] = rates[0]
    for n in range(2):
        own[COUNT, 2 + n : 3 + n, 0:64] = plans[n, 0].astype(jnp.float32)
        for k in range(2):
            row = 4 + 2 * n + k
            own[COUNT, row : row + 1, 0:64] = seen[n, k, 0]
    odd = lax.axis_index("gx") & 1
    for g in range(COUNT):
        far[g] = own[g, pl.ds(pl.multiple_of(8 * odd, 8), 8), :]
        near[g] = own[g, pl.ds(pl.multiple_of(8 - 8 * odd, 8), 8), :]
    base = {name: GROUPS[name][0] for name in ORDER}

    def rows_of(name, row):
        return [own[base[name] + layer, row : row + 1, :] for layer in range(GROUPS[name][1])]

    blank = jnp.zeros((1, 128), jnp.float32)
    for_next = [jnp.concatenate(rows_of("p", 7) + rows_of("tx", 7), axis=0)]
    for_next += [jnp.zeros((8, 128), jnp.float32)] * 2
    for_prev = [
        jnp.concatenate(rows_of("p", 8) + rows_of("tx", 8), axis=0),
        jnp.concatenate(rows_of("ty", 8) + rows_of("tz", 8) + [blank], axis=0),
        jnp.concatenate(rows_of("pv", 8) + rows_of("p", 9), axis=0),
    ]
    for k in range(3):
        far[COUNT + k] = jnp.where(odd == 1, for_next[k], for_prev[k])
        near[COUNT + k] = jnp.where(odd == 1, for_prev[k], for_next[k])
    far[COUNT + 3] = own[COUNT, 0:8, :]
    near[COUNT + 3] = own[COUNT, 0:8, :]


def lanes():
    return lax.broadcasted_iota(jnp.int32, (8, 128), 1)


def in_slot(lane, start):
    return ((lane - start) & 127) < SLOT


def sorted_ends(axis, far, near):
    odd = (lax.axis_index(axis) & 1) == 1

    def before(g):
        return jnp.where(odd, near[g], far[g])

    def after(g):
        return jnp.where(odd, far[g], near[g])

    return before, after


def pack_cols(own, row_far, row_near, far, near):
    low, high = sorted_ends("gx", row_far, row_near)
    odd = lax.axis_index("gy") & 1
    lane = lanes()
    far_cols = [in_slot(lane, SLOT * (j - odd)) for j in range(SLOTS)]
    near_cols = [in_slot(lane, SLOT * (j - 1 + odd)) for j in range(SLOTS)]
    zero = jnp.zeros((8, 128), jnp.float32)
    blocks = []
    for g in range(COUNT):
        blocks.append(lambda g=g: low(g))
        blocks.append(lambda g=g: own[g, 0:8, :])
        blocks.append(lambda g=g: own[g, 8:16, :])
        blocks.append(lambda g=g: high(g))
    blocks.append(lambda: low(COUNT))
    for extra in range(3):
        blocks.append(lambda g=COUNT + extra: high(g))
    for at in range(PACKED):
        far_part, near_part = zero, zero
        for j, block in enumerate(blocks[at * SLOTS : (at + 1) * SLOTS]):
            moved = block()
            if j:
                moved = pltpu.roll(moved, SLOT * j, 1)
            far_part = jnp.where(far_cols[j], moved, far_part)
            near_part = jnp.where(near_cols[j], moved, near_part)
        far[at] = far_part
        near[at] = near_part
    pair = jnp.where(lane < 64, own[COUNT, 0:8, :], pltpu.roll(low(COUNT + 3), 64, 1))
    for out in (far, near):
        out[PACKED] = pair
        out[PACKED + 1] = high(COUNT + 3)


def split3(value):
    hi = value.astype(jnp.bfloat16).astype(jnp.float32)
    rest = value - hi
    mid = rest.astype(jnp.bfloat16).astype(jnp.float32)
    return hi, mid, rest - mid


def scatter_wells(lists, keep, dense, half):
    info = jnp.concatenate(lists, axis=1)
    width = info.shape[1]
    cell = info[0:1].astype(jnp.int32)
    lane = lax.broadcasted_iota(jnp.int32, (1, width), 1)
    base, low, high = keep(lane)
    layer = lax.shift_right_logical(cell, 11)
    row = lax.shift_right_logical(cell, 7) & 15
    col = cell & 127
    place = row + base
    inside = (place >= 8) & (col >= low) & (col < high)
    target = jnp.where(inside, layer * 40 + place - 8, -1)
    rows = lax.broadcasted_iota(jnp.int32, (160, width), 0)
    hit = rows == target
    cols = lax.broadcasted_iota(jnp.int32, (128, width), 0)
    to_col = jnp.where(cols == col, 1.0, 0.0).astype(jnp.bfloat16)
    rate = info[1:2] * 0.5
    values = [
        rate * info[2:3],
        rate * info[3:4],
        info[4:5],
        info[5:6],
        info[6:7],
        info[7:8],
    ]
    dims = (((1,), (1,)), ((), ()))
    for number, value in enumerate(values):
        total = None
        for part in split3(value):
            left = jnp.where(hit, part, 0.0).astype(jnp.bfloat16)
            term = lax.dot_general(left, to_col, dims, preferred_element_type=jnp.float32)
            total = term if total is None else total + term
        for k in range(4):
            dense[number, k, half, 8:48, :] = total[k * 40 : k * 40 + 40]
    left = jnp.where(hit, 1.0, 0.0).astype(jnp.bfloat16)
    total = lax.dot_general(left, to_col, dims, preferred_element_type=jnp.float32)
    for k in range(4):
        dense[6, k, half, 8:48, :] = total[k * 40 : k * 40 + 40]


SRC0, SRC1, OP0, OS0, OP1, OS1, CNT = range(7)


def model(
    own, row_far, row_near, col_far, col_near,
    grad_x, grad_y, grad_z,
    fld, dense, upi, rcp, tym, q0, p1, q1, p2, f0, d0, s1, f1, d1, fup0, fup1, dp1, dp2,
    sig2, psi2, psi1, mup2, muq1, mup1, muq0, flux, rest,
):
    low, high = sorted_ends("gx", row_far, row_near)
    from_prev, from_next = sorted_ends("gy", col_far, col_near)
    lane = lanes()
    at_end = lane == 127
    at_start = lane == 0
    odd_col = lax.axis_index("gy") & 1
    far_cols = [in_slot(lane, SLOT * (j - 1 + odd_col)) for j in range(SLOTS)]

    def unpack(piece):
        at, j = piece // SLOTS, piece % SLOTS
        both = jnp.where(far_cols[j], col_far[at], col_near[at])
        return pltpu.roll(both, 128 - SLOT * j, 1) if j else both

    for name in ORDER:
        first, layers = GROUPS[name]
        for layer in range(layers):
            g = first + layer
            center = [
                low(g),
                own[g, 0:8, :],
                own[g, 8:16, :],
                high(g),
            ]
            halo = [unpack(g * 4 + k) for k in range(4)]
            for k in range(4):
                rows = slice(8 + 8 * k, 16 + 8 * k)
                if name == "up":
                    upi[layer, 0, rows, :] = center[k].astype(jnp.int32)
                    upi[layer, 1, rows, :] = halo[k].astype(jnp.int32)
                else:
                    fld[g, 0, rows, :] = center[k]
                    fld[g, 1, rows, :] = halo[k]
    PB, SB, XB, YB, ZB, VB = (GROUPS[name][0] for name in ORDER[:6])
    extras = [
        (low(COUNT), unpack(COUNT * 4), [(PB, 7), (XB, 7)]),
        (high(COUNT), unpack(COUNT * 4 + 1), [(PB, 40), (XB, 40)]),
        (high(COUNT + 1), unpack(COUNT * 4 + 2), [(YB, 40), (ZB, 40)]),
        (high(COUNT + 2), unpack(COUNT * 4 + 3), [(VB, 40), (PB, 41)]),
    ]
    for center, halo, places in extras:
        for block, (base, row) in enumerate(places):
            for layer in range(3 if base == ZB else 4):
                k = 4 * block + layer
                fld[base + layer, 0, row : row + 1, :] = center[k : k + 1]
                fld[base + layer, 1, row : row + 1, :] = halo[k : k + 1]

    def across(at):
        return [at(PACKED), at(PACKED + 1)[:, 0:64]]

    scatter_wells(
        [own[COUNT, 0:8, 0:64], low(COUNT + 3)[:, 0:64], high(COUNT + 3)[:, 0:64]],
        lambda w: (jnp.where(w < 64, 16, jnp.where(w < 128, 0, 32)), 0, 128),
        dense,
        0,
    )

    def beside(w):
        within = jnp.where(w >= 192, w - 192, w)
        base = jnp.where(within < 64, 16, jnp.where(within < 128, 0, 32))
        return base, jnp.where(w < 192, 128 - SLOT, 0), jnp.where(w < 192, 128, SLOT)

    scatter_wells(across(from_prev) + across(from_next), beside, dense, 1)

    def here(ref, k, t):
        rows = slice(8 * t, 8 * t + 8)
        return ref[k, 0, rows, :], ref[k, 1, rows, :]

    def down(ref, k, t):
        rows = slice(8 * t + 1, 8 * t + 9)
        return ref[k, 0, rows, :], ref[k, 1, rows, :]

    def above(ref, k, t):
        rows = slice(8 * t - 1, 8 * t + 7)
        return ref[k, 0, rows, :], ref[k, 1, rows, :]

    def put(ref, k, t, pair):
        rows = slice(8 * t, 8 * t + 8)
        ref[k, 0, rows, :] = pair[0]
        ref[k, 1, rows, :] = pair[1]

    def right(pair):
        a, b = pltpu.roll(pair[0], 127, 1), pltpu.roll(pair[1], 127, 1)
        return jnp.where(at_end, b, a), jnp.where(at_end, a, b)

    def left(pair):
        a, b = pltpu.roll(pair[0], 1, 1), pltpu.roll(pair[1], 1, 1)
        return jnp.where(at_start, b, a), jnp.where(at_start, a, b)

    def both(f, *pairs):
        return tuple(f(*(pair[h] for pair in pairs)) for h in range(2))

    def add(a, b):
        return both(lambda x, y: x + y, a, b)

    def sub(a, b):
        return both(lambda x, y: x - y, a, b)

    def mul(a, b):
        return both(lambda x, y: x * y, a, b)

    for t in range(1, 6):
        for k in range(4):
            volume = here(fld, VB + k, t)
            beyond = right(volume)
            put(fld, YB + k, t, both(lambda v, y: jnp.where(v == 0.0, 0.0, y), beyond, here(fld, YB + k, t)))
    for k in range(4):
        volume_below = fld[VB + k, 0, 32:33, :], fld[VB + k, 1, 32:33, :]
        for h in range(2):
            fld[XB + k, h, 31:32, :] = jnp.where(volume_below[h] == 0.0, 0.0, fld[XB + k, h, 31:32, :])
    for t in range(1, 6):
        for k in range(4):
            volume = both(lambda v: jnp.where(v == 0.0, 1.0, v), here(fld, VB + k, t))
            put(fld, VB + k, t, volume)
            west = left(here(fld, YB + k, t))
            put(tym, k, t, west)
            total = add(volume, add(here(fld, XB + k, t), above(fld, XB + k, t)))
            total = add(total, add(here(fld, YB + k, t), west))
            if k < 3:
                total = add(total, here(fld, ZB + k, t))
            if k > 0:
                total = add(total, here(fld, ZB + k - 1, t))
            put(rcp, k, t, both(lambda v: 1.0 / v, total))

    def neighbours(ref, base, k, t):
        value = here(ref, base + k, t)
        total = mul(here(fld, XB + k, t), down(ref, base + k, t))
        total = add(total, mul(above(fld, XB + k, t), above(ref, base + k, t)))
        total = add(total, mul(here(fld, YB + k, t), right(value)))
        total = add(total, mul(here(tym, k, t), left(value)))
        if k < 3:
            total = add(total, mul(here(fld, ZB + k, t), here(ref, base + k + 1, t)))
        if k > 0:
            total = add(total, mul(here(fld, ZB + k - 1, t), here(ref, base + k - 1, t)))
        return total

    def relax(out, ref, base, old, old_base, source, tiles):
        for t in tiles:
            for k in range(4):
                total = add(
                    mul(here(fld, VB + k, t), here(old, old_base + k, t)), here(dense.at[source], k, t)
                )
                total = add(total, neighbours(ref, base, k, t))
                put(out, k, t, mul(total, here(rcp, k, t)))

    def mobility(value):
        rest_of = 1.0 - value
        wetted = value * value
        inverse = 1.0 / (wetted + 0.5 * rest_of * rest_of)
        return wetted * inverse, value * rest_of * inverse * inverse

    def put_mobility(value, k, t, mobile, slope):
        pairs = [mobility(v) for v in value]
        put(mobile, k, t, (pairs[0][0], pairs[1][0]))
        put(slope, k, t, (pairs[0][1], pairs[1][1]))

    def bit(k, t, number):
        return both(lambda v: (v & (1 << number)) != 0, here(upi, k, t))

    def choose(mask, a, b):
        return both(lambda m, x, y: jnp.where(m, x, y), mask, a, b)

    def transport(pressure, sat, sat_base, mobile, n, fup, dp, finish):
        for t in range(1, 5):
            below = None
            for k in range(4):
                mob = here(mobile, k, t)
                pres = here(pressure, k, t)
                drop_x = sub(pres, down(pressure, k, t))
                drop_y = sub(pres, right(pres))
                up_x = choose(bit(k, t, 3 * n), mob, down(mobile, k, t))
                up_y = choose(bit(k, t, 3 * n + 1), mob, right(mob))
                put(fup, k, t, up_x)
                put(fup, 4 + k, t, up_y)
                put(dp, k, t, drop_x)
                put(dp, 4 + k, t, drop_y)
                flux_x = mul(mul(here(fld, XB + k, t), up_x), drop_x)
                flux_y = mul(mul(here(fld, YB + k, t), up_y), drop_y)
                put(flux, k, t, flux_x)
                net = add(sub(flux_x, above(flux, k, t)), sub(flux_y, left(flux_y)))
                if k < 3:
                    drop_z = sub(pres, here(pressure, k + 1, t))
                    up_z = choose(bit(k, t, 3 * n + 2), mob, here(mobile, k + 1, t))
                    put(fup, 8 + k, t, up_z)
                    put(dp, 8 + k, t, drop_z)
                    flux_z = mul(mul(here(fld, ZB + k, t), up_z), drop_z)
                    net = add(net, flux_z)
                if k > 0:
                    net = sub(net, below)
                below = flux_z
                moved = both(
                    lambda o, f, v: o - time_step * f / v,
                    here(sat, sat_base + k, t),
                    net,
                    here(fld, VB + k, t),
                )
                finish(moved, k, t)

    tiles = range(1, 5)
    relax(q0, fld, PB, fld, PB, SRC0, range(1, 6))
    relax(p1, q0, 0, fld, PB, SRC0, tiles)
    for t in tiles:
        for k in range(4):
            put_mobility(here(fld, SB + k, t), k, t, f0, d0)

    def finish_first(moved, k, t):
        put(s1, k, t, moved)
        put_mobility(moved, k, t, f1, d1)

    transport(p1, fld, SB, f0, 0, fup0, dp1, finish_first)
    relax(q1, p1, 0, p1, 0, SRC1, tiles)
    relax(p2, q1, 0, p1, 0, SRC1, tiles)

    def finish_second(moved, k, t):
        miss = sub(mul(here(dense.at[CNT], k, t), moved), here(dense.at[OS1], k, t))
        put(sig2, k, t, miss)
        put(psi2, k, t, both(lambda m, v: time_step * m / v, miss, here(fld, VB + k, t)))

    transport(p2, s1, 0, f1, 1, fup1, dp2, finish_second)

    for t in tiles:
        below_h = below_r = None
        for k in range(4):
            psi = here(psi2, k, t)
            phi_x = mul(sub(down(psi2, k, t), psi), here(fld, XB + k, t))
            phi_y = mul(sub(right(psi), psi), here(fld, YB + k, t))
            h_x = mul(phi_x, here(fup1, k, t))
            h_y = mul(phi_y, here(fup1, 4 + k, t))
            k_x = mul(phi_x, here(dp2, k, t))
            k_y = mul(phi_y, here(dp2, 4 + k, t))
            zero = (jnp.zeros((8, 128), jnp.float32),) * 2
            s_x = choose(bit(k, t, 3), k_x, zero)
            s_y = choose(bit(k, t, 4), k_y, zero)
            r_x = sub(k_x, s_x)
            r_y = sub(k_y, s_y)
            put(flux, k, t, h_x)
            put(rest, k, t, r_x)
            press = add(sub(h_x, above(flux, k, t)), sub(h_y, left(h_y)))
            satur = add(add(s_x, above(rest, k, t)), add(s_y, left(r_y)))
            if k < 3:
                phi_z = mul(sub(here(psi2, k + 1, t), psi), here(fld, ZB + k, t))
                h_z = mul(phi_z, here(fup1, 8 + k, t))
                k_z = mul(phi_z, here(dp2, 8 + k, t))
                s_z = choose(bit(k, t, 5), k_z, zero)
                press = add(press, h_z)
                satur = add(satur, s_z)
            if k > 0:
                press = sub(press, below_h)
                satur = add(satur, below_r)
            if k < 3:
                below_h, below_r = h_z, sub(k_z, s_z)
            count = here(dense.at[CNT], k, t)
            press = add(press, sub(mul(count, here(p2, k, t)), here(dense.at[OP1], k, t)))
            put(mup2, k, t, mul(press, here(rcp, k, t)))
            sigma = add(here(sig2, k, t), mul(satur, here(d1, k, t)))
            sigma = add(sigma, sub(mul(count, here(s1, k, t)), here(dense.at[OS0], k, t)))
            put(psi1, k, t, both(lambda m, v: time_step * m / v, sigma, here(fld, VB + k, t)))

    for t in tiles:
        for k in range(4):
            put(muq1, k, t, mul(neighbours(mup2, 0, k, t), here(rcp, k, t)))

    for t in tiles:
        below_h = None
        for k in range(4):
            psi = here(psi1, k, t)
            h_x = mul(mul(sub(down(psi1, k, t), psi), here(fld, XB + k, t)), here(fup0, k, t))
            h_y = mul(mul(sub(right(psi), psi), here(fld, YB + k, t)), here(fup0, 4 + k, t))
            put(flux, k, t, h_x)
            press = add(sub(h_x, above(flux, k, t)), sub(h_y, left(h_y)))
            if k < 3:
                h_z = mul(mul(sub(here(psi1, k + 1, t), psi), here(fld, ZB + k, t)), here(fup0, 8 + k, t))
                press = add(press, h_z)
            if k > 0:
                press = sub(press, below_h)
            below_h = h_z
            count = here(dense.at[CNT], k, t)
            press = add(press, sub(mul(count, here(p1, k, t)), here(dense.at[OP0], k, t)))
            carried = mul(here(fld, VB + k, t), add(here(mup2, k, t), here(muq1, k, t)))
            press = add(press, add(carried, neighbours(muq1, 0, k, t)))
            put(mup1, k, t, mul(press, here(rcp, k, t)))

    for t in range(2, 5):
        for k in range(4):
            put(muq0, k, t, mul(neighbours(mup1, 0, k, t), here(rcp, k, t)))

    stages = (
        (mup2, q1, 0, p2, 0),
        (muq1, p1, 0, q1, 0),
        (mup1, q0, 0, p1, 0),
        (muq0, fld, PB, q0, 0),
    )
    for t in range(2, 4):
        rows = slice(8 * t - 16, 8 * t - 8)
        for k in range(4):
            sum_x = sum_y = sum_z = None
            for mu, value, value_base, out, out_base in stages:
                mu_c, v_c, o_c = here(mu, k, t), here(value, value_base + k, t), here(out, out_base + k, t)
                mu_d, v_d, o_d = down(mu, k, t), down(value, value_base + k, t), down(out, out_base + k, t)
                term = mu_c[0] * (v_d[0] - o_c[0]) + mu_d[0] * (v_c[0] - o_d[0])
                sum_x = term if sum_x is None else sum_x + term
                mu_r, v_r, o_r = right(mu_c), right(v_c), right(o_c)
                term = mu_c[0] * (v_r[0] - o_c[0]) + mu_r[0] * (v_c[0] - o_r[0])
                sum_y = term if sum_y is None else sum_y + term
                if k < 3:
                    mu_u = here(mu, k + 1, t)
                    v_u = here(value, value_base + k + 1, t)
                    o_u = here(out, out_base + k + 1, t)
                    term = mu_c[0] * (v_u[0] - o_c[0]) + mu_u[0] * (v_c[0] - o_u[0])
                    sum_z = term if sum_z is None else sum_z + term
            for psi, fup, dp in ((psi2, fup1, dp2), (psi1, fup0, dp1)):
                mid = here(psi, k, t)
                phi = down(psi, k, t)[0] - mid[0]
                sum_x = sum_x + phi * here(fup, k, t)[0] * here(dp, k, t)[0]
                phi = right(mid)[0] - mid[0]
                sum_y = sum_y + phi * here(fup, 4 + k, t)[0] * here(dp, 4 + k, t)[0]
                if k < 3:
                    phi = here(psi, k + 1, t)[0] - mid[0]
                    sum_z = sum_z + phi * here(fup, 8 + k, t)[0] * here(dp, 8 + k, t)[0]
            grad_x[k, rows, :] = jnp.where(here(fld, XB + k, t)[0] == 0.0, 0.0, sum_x)
            grad_y[k, rows, :] = jnp.where(here(fld, YB + k, t)[0] == 0.0, 0.0, sum_y)
            if k < 3:
                grad_z[k, rows, :] = sum_z


def swapped(value, axis, first):
    count = lax.axis_size(axis)
    pairs = []
    for i in range(first, count - 1, 2):
        pairs += [(i, i + 1), (i + 1, i)]
    return lax.ppermute(value, axis, pairs)


def on_device(p, s, tx, ty, tz, pv, up, cell, rate, plan, observed):
    f32 = jnp.float32

    def shape(*dims):
        return jax.ShapeDtypeStruct(dims, f32)

    limit = pltpu.CompilerParams(vmem_limit_bytes=48 * 1024 * 1024)
    inputs = (p, s, tx, ty, tz, pv, up, cell, rate, plan, observed)
    inputs = [pltpu.with_memory_space_constraint(value, pltpu.HBM) for value in inputs]
    strip = shape(COUNT + 4, 8, 128)
    own, far, near = pl.pallas_call(
        pack_rows,
        out_shape=(shape(COUNT + 1, 16, 128), strip, strip),
        in_specs=[pl.BlockSpec(memory_space=pltpu.HBM)] * len(inputs),
        scratch_shapes=[pltpu.VMEM(value.shape, value.dtype) for value in inputs[6:]]
        + [pltpu.SemaphoreType.DMA((len(inputs),))],
        compiler_params=limit,
        name="pack_rows",
    )(*inputs)
    row_far = swapped(far, "gx", 1)
    row_near = swapped(near, "gx", 0)
    strip = shape(PACKED + 2, 8, 128)
    far, near = pl.pallas_call(
        pack_cols,
        out_shape=(strip, strip),
        compiler_params=limit,
        name="pack_cols",
    )(own, row_far, row_near)
    col_far = swapped(far, "gy", 1)
    col_near = swapped(near, "gy", 0)

    def cells(count, dtype=f32):
        return pltpu.VMEM((count, 2, 56, 128), dtype)

    scratch = [cells(23), pltpu.VMEM((7, 4, 2, 56, 128), f32), cells(4, jnp.int32)]
    scratch += [cells(4) for _ in range(11)]
    scratch += [cells(11) for _ in range(4)]
    scratch += [cells(4) for _ in range(9)]
    return pl.pallas_call(
        model,
        out_shape=(shape(*tx.shape), shape(*ty.shape), shape(*tz.shape)),
        scratch_shapes=scratch,
        compiler_params=limit,
        name="model",
    )(own, row_far, row_near, col_far, col_near)


def solution(mesh):
    cells = P(None, "gx", "gy")
    in_specs = (cells,) * 7 + (
        P("gx", "gy", None),
        P("gx", "gy", None),
        P(None, "gx", "gy", None),
        P(None, None, "gx", "gy", None),
    )
    return jax.shard_map(
        on_device, mesh=mesh, in_specs=in_specs, out_specs=(cells,) * 3, check_vma=False
    )
```

profile of v0, /device:TPU:0, one launch (start us, length us, event | category | flops | bytes accessed | tf_op | source)
XLA Modules:
  0.0 19.0 jit_solution(12169980480708516818)
XLA Ops:
  0.6 1.0 %pack_rows.1 = (f32[28,16,128]{2,1,0:T(8,128)S(1)}, f32[31,8,128]{2,1,0:T(8,128)S(1)}, f32[31,8,128]{2,1,0:T(8,128)S(1)}) custom-call(f32[4,16,128]{2,1,0:T(8,128)} %refs_0_.1, f32[4,16,128]{2,1,0:T(8,128)} %refs_1_.1, f32[4,16,128]{2,1,0:T(8,128)} %refs_2_.1, f32[4,16,128]{2,1,0:T(8,128)} %refs_3_.1, f32[3,16,128]{2,1,0:T(8,128)} %refs_4_.1, ...), custom_call_target="tpu_custom_call" | custom-call | tf_op jit(solution)/shard_map/pack_rows/pallas_call | solution.py:519
  1.6 0.7 %collective-permute-start = (f32[31,8,128]{2,1,0:T(8,128)S(1)}, f32[31,8,128]{2,1,0:T(8,128)S(1)}, u32[]{:S(2)}, u32[]{:S(2)}) collective-permute-start(f32[31,8,128]{2,1,0:T(8,128)S(1)} %get-tuple-element.9), channel_id=1, source_target_pairs={{4,8},{8,4},{12,16},{16,12},{20,24},{24,20},{5,9},{9,5},{13,17},{1... | collective-permute-start | bytes 380936 | tf_op jit(solution)/shard_map/ppermute | solution.py:506
  2.3 4.4 %collective-permute-start.1 = (f32[31,8,128]{2,1,0:T(8,128)S(1)}, f32[31,8,128]{2,1,0:T(8,128)S(1)}, u32[]{:S(2)}, u32[]{:S(2)}) collective-permute-start(f32[31,8,128]{2,1,0:T(8,128)S(1)} %get-tuple-element.10), channel_id=1, source_target_pairs={{0,4},{4,0},{8,12},{12,8},{16,20},{20,16},{24,28},{28,24},{1,5},{5... | collective-permute-start | bytes 380936 | tf_op jit(solution)/shard_map/ppermute | solution.py:506
  6.8 0.0 collective-permute-done.row_far
  6.8 1.0 %collective-permute-done.1.row_near = f32[31,8,128]{2,1,0:T(8,128)S(1)} collective-permute-done((f32[31,8,128]{2,1,0:T(8,128)S(1)}, f32[31,8,128]{2,1,0:T(8,128)S(1)}, u32[]{:S(2)}, u32[]{:S(2)}) %collective-permute-start.1) | collective-permute-done | bytes 127008 | tf_op jit(solution)/shard_map/ppermute | solution.py:506
  7.7 0.2 pack_cols.1
  7.9 0.7 %collective-permute-start.2 = (f32[12,8,128]{2,1,0:T(8,128)S(1)}, f32[12,8,128]{2,1,0:T(8,128)S(1)}, u32[]{:S(2)}, u32[]{:S(2)}) collective-permute-start(f32[12,8,128]{2,1,0:T(8,128)S(1)} %get-tuple-element.11), channel_id=1, source_target_pairs={{1,2},{2,1},{5,6},{6,5},{9,10},{10,9},{13,14},{14,13},{17,18},{18,... | collective-permute-start | bytes 147464 | tf_op jit(solution)/shard_map/ppermute | solution.py:506
  8.6 4.3 %collective-permute-start.3 = (f32[12,8,128]{2,1,0:T(8,128)S(1)}, f32[12,8,128]{2,1,0:T(8,128)S(1)}, u32[]{:S(2)}, u32[]{:S(2)}) collective-permute-start(f32[12,8,128]{2,1,0:T(8,128)S(1)} %get-tuple-element.12), channel_id=1, source_target_pairs={{0,1},{1,0},{2,3},{3,2},{4,5},{5,4},{6,7},{7,6},{8,9},{9,8},{10,11... | collective-permute-start | bytes 147464 | tf_op jit(solution)/shard_map/ppermute | solution.py:506
  12.9 0.0 collective-permute-done.2.col_far
  12.9 3.0 %collective-permute-done.3.col_near = f32[12,8,128]{2,1,0:T(8,128)S(1)} collective-permute-done((f32[12,8,128]{2,1,0:T(8,128)S(1)}, f32[12,8,128]{2,1,0:T(8,128)S(1)}, u32[]{:S(2)}, u32[]{:S(2)}) %collective-permute-start.3) | collective-permute-done | bytes 49184 | tf_op jit(solution)/shard_map/ppermute | solution.py:506
  15.9 3.1 %model.1 = (f32[4,16,128]{2,1,0:T(8,128)}, f32[4,16,128]{2,1,0:T(8,128)}, f32[3,16,128]{2,1,0:T(8,128)}) custom-call(f32[28,16,128]{2,1,0:T(8,128)S(1)} %get-tuple-element.8.own, f32[31,8,128]{2,1,0:T(8,128)S(1)} %collective-permute-done.row_far, f32[31,8,128]{2,1,0:T(8,128)S(1)} %collective-permute-done.1.row_near, ...), custom_call_target="tpu_custom_call" | custom-call | tf_op jit(solution)/shard_map/model/pallas_call | solution.py:547
Async XLA Ops:
  1.6 5.1 %collective-permute-start = (f32[31,8,128]{2,1,0:T(8,128)S(1)}, f32[31,8,128]{2,1,0:T(8,128)S(1)}, u32[]{:S(2)}, u32[]{:S(2)}) collective-permute-start(f32[31,8,128]{2,1,0:T(8,128)S(1)} %get-tuple-element.9), channel_id=1, source_target_pairs={{4,8},{8,4},{12,16},{16,12},{20,24},{24,20},{5,9},{9,5},{13,17},{1... | collective-permute-start | bytes 380936 | tf_op jit(solution)/shard_map/ppermute | solution.py:506
  2.3 5.4 %collective-permute-start.1 = (f32[31,8,128]{2,1,0:T(8,128)S(1)}, f32[31,8,128]{2,1,0:T(8,128)S(1)}, u32[]{:S(2)}, u32[]{:S(2)}) collective-permute-start(f32[31,8,128]{2,1,0:T(8,128)S(1)} %get-tuple-element.10), channel_id=1, source_target_pairs={{0,4},{4,0},{8,12},{12,8},{16,20},{20,16},{24,28},{28,24},{1,5},{5... | collective-permute-start | bytes 380936 | tf_op jit(solution)/shard_map/ppermute | solution.py:506
  7.9 5.0 %collective-permute-start.2 = (f32[12,8,128]{2,1,0:T(8,128)S(1)}, f32[12,8,128]{2,1,0:T(8,128)S(1)}, u32[]{:S(2)}, u32[]{:S(2)}) collective-permute-start(f32[12,8,128]{2,1,0:T(8,128)S(1)} %get-tuple-element.11), channel_id=1, source_target_pairs={{1,2},{2,1},{5,6},{6,5},{9,10},{10,9},{13,14},{14,13},{17,18},{18,... | collective-permute-start | bytes 147464 | tf_op jit(solution)/shard_map/ppermute | solution.py:506
  8.6 7.3 %collective-permute-start.3 = (f32[12,8,128]{2,1,0:T(8,128)S(1)}, f32[12,8,128]{2,1,0:T(8,128)S(1)}, u32[]{:S(2)}, u32[]{:S(2)}) collective-permute-start(f32[12,8,128]{2,1,0:T(8,128)S(1)} %get-tuple-element.12), channel_id=1, source_target_pairs={{0,1},{1,0},{2,3},{3,2},{4,5},{5,4},{6,7},{7,6},{8,9},{9,8},{10,11... | collective-permute-start | bytes 147464 | tf_op jit(solution)/shard_map/ppermute | solution.py:506
where the time goes:
time: 19.2 us; the launch traced here: 19 us
  starting transfers between devices  10.1 us (53%)
  Pallas kernels  4.29 us (22%)
  waiting for transfers between devices  4.01 us (21%)
  between operations  0.67 us (3%)
    ppermute x4, starting transfers between devices, swapped(): return lax.ppermute(value, axis, pairs)  10.1 us
    ppermute x4, waiting for transfers between devices, swapped(): return lax.ppermute(value, axis, pairs)  4.01 us
    pallas_call x1, Pallas kernels, on_device(): pl.pallas_call(model, out_shape=(shape(*tx.shape), shape(*ty.shape), shap...  3.11 us
    pallas_call x1, Pallas kernels, on_device(): pl.pallas_call(pack_rows, out_shape=(shape(COUNT + 1, 16, 128), strip, st...  1 us
  transfers between devices with their start and end apart: 4, of which 2 were waited for; matrix products, arithmetic and copies ran while one was open for 0% of the time, Pallas kernels for 0%

commit v1 on v0

--- a/solution.py
+++ b/solution.py
@@ -12,16 +12,23 @@
 COUNT = 27
 SLOT = 10
 SLOTS = 12
-PIECES = COUNT * 4 + 4
-PACKED = -(-PIECES // SLOTS)
+PACKED = 3
+
+
+def lanes():
+    return lax.broadcasted_iota(jnp.int32, (8, 128), 1)
+
+
+def in_slot(lane, start):
+    return ((lane - start) & 127) < SLOT
 
 
 FIELDS = 11
 
 
-def pack_rows(*refs):
+def pack_tile(*refs):
     p, s, tx, ty, tz, pv, up, cell, rate, plan, observed = refs[:FIELDS]
-    own, far, near, upi, cells, rates, plans, seen, sems = refs[FIELDS:]
+    own, col_far, col_near, far, near, upi, cells, rates, plans, seen, sems = refs[FIELDS:]
     targets = [own.at[pl.ds(*GROUPS[name])] for name in ORDER[:6]] + [upi, cells, rates, plans, seen]
     copies = [
         pltpu.make_async_copy(source, target, sems.at[k])
@@ -64,14 +71,22 @@
         near[COUNT + k] = jnp.where(odd == 1, for_prev[k], for_next[k])
     far[COUNT + 3] = own[COUNT, 0:8, :]
     near[COUNT + 3] = own[COUNT, 0:8, :]
-
-
-def lanes():
-    return lax.broadcasted_iota(jnp.int32, (8, 128), 1)
-
-
-def in_slot(lane, start):
-    return ((lane - start) & 127) < SLOT
+    odd_col = lax.axis_index("gy") & 1
+    lane = lanes()
+    far_cols = [in_slot(lane, SLOT * (j - odd_col)) for j in range(SLOTS)]
+    near_cols = [in_slot(lane, SLOT * (j - 1 + odd_col)) for j in range(SLOTS)]
+    for half, beyond in ((0, for_prev), (1, for_next[:1])):
+        blocks = [own[g, 8 * half : 8 * half + 8, :] for g in range(COUNT)] + beyond
+        for at in range(PACKED):
+            far_part = near_part = jnp.zeros((8, 128), jnp.float32)
+            for j, block in enumerate(blocks[at * SLOTS : (at + 1) * SLOTS]):
+                moved = pltpu.roll(block, SLOT * j, 1) if j else block
+                far_part = jnp.where(far_cols[j], moved, far_part)
+                near_part = jnp.where(near_cols[j], moved, near_part)
+            col_far[PACKED * half + at] = far_part
+            col_near[PACKED * half + at] = near_part
+    col_far[2 * PACKED] = own[COUNT, 0:8, :]
+    col_near[2 * PACKED] = own[COUNT, 0:8, :]
 
 
 def sorted_ends(axis, far, near):
@@ -86,36 +101,16 @@
     return before, after
 
 
-def pack_cols(own, row_far, row_near, far, near):
-    low, high = sorted_ends("gx", row_far, row_near)
-    odd = lax.axis_index("gy") & 1
-    lane = lanes()
-    far_cols = [in_slot(lane, SLOT * (j - odd)) for j in range(SLOTS)]
-    near_cols = [in_slot(lane, SLOT * (j - 1 + odd)) for j in range(SLOTS)]
-    zero = jnp.zeros((8, 128), jnp.float32)
-    blocks = []
-    for g in range(COUNT):
-        blocks.append(lambda g=g: low(g))
-        blocks.append(lambda g=g: own[g, 0:8, :])
-        blocks.append(lambda g=g: own[g, 8:16, :])
-        blocks.append(lambda g=g: high(g))
-    blocks.append(lambda: low(COUNT))
-    for extra in range(3):
-        blocks.append(lambda g=COUNT + extra: high(g))
+def pack_corners(col_far, col_near, far, near):
+    before, after = sorted_ends("gy", col_far, col_near)
+    odd = lax.axis_index("gx") & 1
     for at in range(PACKED):
-        far_part, near_part = zero, zero
-        for j, block in enumerate(blocks[at * SLOTS : (at + 1) * SLOTS]):
-            moved = block()
-            if j:
-                moved = pltpu.roll(moved, SLOT * j, 1)
-            far_part = jnp.where(far_cols[j], moved, far_part)
-            near_part = jnp.where(near_cols[j], moved, near_part)
-        far[at] = far_part
-        near[at] = near_part
-    pair = jnp.where(lane < 64, own[COUNT, 0:8, :], pltpu.roll(low(COUNT + 3), 64, 1))
-    for out in (far, near):
-        out[PACKED] = pair
-        out[PACKED + 1] = high(COUNT + 3)
+        for out, first in ((far, PACKED * odd), (near, PACKED - PACKED * odd)):
+            out[at] = after(first + at)
+            out[PACKED + at] = before(first + at)
+    both = jnp.where(lanes() < 64, before(2 * PACKED), pltpu.roll(after(2 * PACKED), 64, 1))
+    far[2 * PACKED] = both
+    near[2 * PACKED] = both
 
 
 def split3(value):
@@ -169,23 +164,31 @@
 
 
 def model(
-    own, row_far, row_near, col_far, col_near,
+    col_far, col_near, corner_far, corner_near, row_far, row_near, own,
     grad_x, grad_y, grad_z,
     fld, dense, upi, rcp, tym, q0, p1, q1, p2, f0, d0, s1, f1, d1, fup0, fup1, dp1, dp2,
     sig2, psi2, psi1, mup2, muq1, mup1, muq0, flux, rest,
 ):
     low, high = sorted_ends("gx", row_far, row_near)
-    from_prev, from_next = sorted_ends("gy", col_far, col_near)
+    before, after = sorted_ends("gy", col_far, col_near)
+    low_corner, high_corner = sorted_ends("gx", corner_far, corner_near)
     lane = lanes()
     at_end = lane == 127
     at_start = lane == 0
     odd_col = lax.axis_index("gy") & 1
     far_cols = [in_slot(lane, SLOT * (j - 1 + odd_col)) for j in range(SLOTS)]
-
-    def unpack(piece):
-        at, j = piece // SLOTS, piece % SLOTS
-        both = jnp.where(far_cols[j], col_far[at], col_near[at])
-        return pltpu.roll(both, 128 - SLOT * j, 1) if j else both
+    first_cols = [in_slot(lane, SLOT * j) for j in range(SLOTS)]
+
+    def back(value, j):
+        return pltpu.roll(value, 128 - SLOT * j, 1) if j else value
+
+    def beside_own(g, half):
+        at, j = PACKED * half + g // SLOTS, g % SLOTS
+        return back(jnp.where(far_cols[j], col_far[at], col_near[at]), j)
+
+    def beside_other(corner, g):
+        at, j = g // SLOTS, g % SLOTS
+        return back(jnp.where(first_cols[j], corner(at), corner(PACKED + at)), j)
 
     for name in ORDER:
         first, layers = GROUPS[name]
@@ -197,7 +200,12 @@
                 own[g, 8:16, :],
                 high(g),
             ]
-            halo = [unpack(g * 4 + k) for k in range(4)]
+            halo = [
+                beside_other(low_corner, g),
+                beside_own(g, 0),
+                beside_own(g, 1),
+                beside_other(high_corner, g),
+            ]
             for k in range(4):
                 rows = slice(8 + 8 * k, 16 + 8 * k)
                 if name == "up":
@@ -208,10 +216,10 @@
                     fld[g, 1, rows, :] = halo[k]
     PB, SB, XB, YB, ZB, VB = (GROUPS[name][0] for name in ORDER[:6])
     extras = [
-        (low(COUNT), unpack(COUNT * 4), [(PB, 7), (XB, 7)]),
-        (high(COUNT), unpack(COUNT * 4 + 1), [(PB, 40), (XB, 40)]),
-        (high(COUNT + 1), unpack(COUNT * 4 + 2), [(YB, 40), (ZB, 40)]),
-        (high(COUNT + 2), unpack(COUNT * 4 + 3), [(VB, 40), (PB, 41)]),
+        (low(COUNT), beside_other(low_corner, COUNT), [(PB, 7), (XB, 7)]),
+        (high(COUNT), beside_other(high_corner, COUNT + 0), [(PB, 40), (XB, 40)]),
+        (high(COUNT + 1), beside_other(high_corner, COUNT + 1), [(YB, 40), (ZB, 40)]),
+        (high(COUNT + 2), beside_other(high_corner, COUNT + 2), [(VB, 40), (PB, 41)]),
     ]
     for center, halo, places in extras:
         for block, (base, row) in enumerate(places):
@@ -220,9 +228,6 @@
                 fld[base + layer, 0, row : row + 1, :] = center[k : k + 1]
                 fld[base + layer, 1, row : row + 1, :] = halo[k : k + 1]
 
-    def across(at):
-        return [at(PACKED), at(PACKED + 1)[:, 0:64]]
-
     scatter_wells(
         [own[COUNT, 0:8, 0:64], low(COUNT + 3)[:, 0:64], high(COUNT + 3)[:, 0:64]],
         lambda w: (jnp.where(w < 64, 16, jnp.where(w < 128, 0, 32)), 0, 128),
@@ -231,11 +236,14 @@
     )
 
     def beside(w):
-        within = jnp.where(w >= 192, w - 192, w)
-        base = jnp.where(within < 64, 16, jnp.where(within < 128, 0, 32))
-        return base, jnp.where(w < 192, 128 - SLOT, 0), jnp.where(w < 192, 128, SLOT)
-
-    scatter_wells(across(from_prev) + across(from_next), beside, dense, 1)
+        block = lax.shift_right_logical(w, 6)
+        base = jnp.where(block < 2, 16, jnp.where(block < 4, 0, 32))
+        ahead = (block & 1) == 1
+        return base, jnp.where(ahead, 0, 128 - SLOT), jnp.where(ahead, SLOT, 128)
+
+    wells = 2 * PACKED
+    lists = [before(wells)[:, 0:64], after(wells)[:, 0:64], low_corner(wells), high_corner(wells)]
+    scatter_wells(lists, beside, dense, 1)
 
     def here(ref, k, t):
         rows = slice(8 * t, 8 * t + 8)
@@ -516,26 +524,29 @@
     inputs = (p, s, tx, ty, tz, pv, up, cell, rate, plan, observed)
     inputs = [pltpu.with_memory_space_constraint(value, pltpu.HBM) for value in inputs]
     strip = shape(COUNT + 4, 8, 128)
-    own, far, near = pl.pallas_call(
-        pack_rows,
-        out_shape=(shape(COUNT + 1, 16, 128), strip, strip),
+    packed = shape(2 * PACKED + 1, 8, 128)
+    own, col_far, col_near, row_far, row_near = pl.pallas_call(
+        pack_tile,
+        out_shape=(shape(COUNT + 1, 16, 128), packed, packed, strip, strip),
         in_specs=[pl.BlockSpec(memory_space=pltpu.HBM)] * len(inputs),
         scratch_shapes=[pltpu.VMEM(value.shape, value.dtype) for value in inputs[6:]]
         + [pltpu.SemaphoreType.DMA((len(inputs),))],
         compiler_params=limit,
-        name="pack_rows",
+        name="pack_tile",
     )(*inputs)
-    row_far = swapped(far, "gx", 1)
-    row_near = swapped(near, "gx", 0)
-    strip = shape(PACKED + 2, 8, 128)
+    col_far = swapped(col_far, "gy", 1)
+    col_near = swapped(col_near, "gy", 0)
+    row_far = swapped(row_far, "gx", 1)
+    row_near = swapped(row_near, "gx", 0)
     far, near = pl.pallas_call(
-        pack_cols,
-        out_shape=(strip, strip),
+        pack_corners,
+        out_shape=(packed, packed),
         compiler_params=limit,
-        name="pack_cols",
-    )(own, row_far, row_near)
-    col_far = swapped(far, "gy", 1)
-    col_near = swapped(near, "gy", 0)
+        cost_estimate=pl.CostEstimate(flops=10**11, bytes_accessed=1 << 28, transcendentals=0),
+        name="pack_corners",
+    )(col_far, col_near)
+    corner_far = swapped(far, "gx", 1)
+    corner_near = swapped(near, "gx", 0)
 
     def cells(count, dtype=f32):
         return pltpu.VMEM((count, 2, 56, 128), dtype)
@@ -550,7 +561,7 @@
         scratch_shapes=scratch,
         compiler_params=limit,
         name="model",
-    )(own, row_far, row_near, col_far, col_near)
+    )(col_far, col_near, corner_far, corner_near, row_far, row_near, own)
 
 
 def solution(mesh):

time: 19.2 us -> 20 us (1.042)
  the two profiles are of different devices: /device:TPU:0 before, /device:TPU:1 now
where the time goes in v1:
time: 20 us; the launch traced here: 19.8 us
  starting transfers between devices  13.2 us (66%)
  Pallas kernels  4.32 us (22%)
  waiting for transfers between devices  1.55 us (8%)
  between operations  0.7 us (4%)
    ppermute x6, starting transfers between devices, swapped(): return lax.ppermute(value, axis, pairs)  13.2 us
    pallas_call x1, Pallas kernels, on_device(): pl.pallas_call(model, out_shape=(shape(*tx.shape), shape(*ty.shape), shap...  3.14 us
    ppermute x6, waiting for transfers between devices, swapped(): return lax.ppermute(value, axis, pairs)  1.55 us
    pallas_call x1, Pallas kernels, on_device(): pl.pallas_call(pack_tile, out_shape=(shape(COUNT + 1, 16, 128), packed, p...  1.1 us
  transfers between devices with their start and end apart: 6, of which 1 were waited for; matrix products, arithmetic and copies ran while one was open for 0% of the time, Pallas kernels for 0%

profile of v1, /device:TPU:1, one launch (start us, length us, event | category | flops | bytes accessed | tf_op | source)
XLA Modules:
  0.0 19.8 jit_solution(14492268322891852797)
XLA Ops:
  0.6 1.1 %pack_tile.1 = (f32[28,16,128]{2,1,0:T(8,128)S(1)}, f32[7,8,128]{2,1,0:T(8,128)S(1)}, f32[7,8,128]{2,1,0:T(8,128)S(1)}, f32[31,8,128]{2,1,0:T(8,128)S(1)}, f32[31,8,128]{2,1,0:T(8,128)S(1)}) custom-call(f32[4,16,128]{2,1,0:T(8,128)} %refs_0_.1, f32[4,16,128]{2,1,0:T(8,128)} %refs_1_.1, f32[4,16,128]{2,1,0:T(8,128)} %refs_2_.1, f32[4,16,128]{2,1,0:T(8,128)} %refs_3_.1, ...), custom_call_target="tpu_custom_call" | custom-call | tf_op jit(solution)/shard_map/pack_tile/pallas_call | solution.py:528
  1.7 0.7 %collective-permute-start = (f32[7,8,128]{2,1,0:T(8,128)S(1)}, f32[7,8,128]{2,1,0:T(8,128)S(1)}, u32[]{:S(2)}, u32[]{:S(2)}) collective-permute-start(f32[7,8,128]{2,1,0:T(8,128)S(1)} %get-tuple-element.10), channel_id=1, source_target_pairs={{1,2},{2,1},{5,6},{6,5},{9,10},{10,9},{13,14},{14,13},{17,18},{18,... | collective-permute-start | bytes 86024 | tf_op jit(solution)/shard_map/ppermute | solution.py:514
  2.4 4.6 %collective-permute-start.1 = (f32[7,8,128]{2,1,0:T(8,128)S(1)}, f32[7,8,128]{2,1,0:T(8,128)S(1)}, u32[]{:S(2)}, u32[]{:S(2)}) collective-permute-start(f32[7,8,128]{2,1,0:T(8,128)S(1)} %get-tuple-element.11), channel_id=1, source_target_pairs={{0,1},{1,0},{2,3},{3,2},{4,5},{5,4},{6,7},{7,6},{8,9},{9,8},{10,11... | collective-permute-start | bytes 86024 | tf_op jit(solution)/shard_map/ppermute | solution.py:514
  7.0 4.3 %collective-permute-start.4 = (f32[31,8,128]{2,1,0:T(8,128)S(1)}, f32[31,8,128]{2,1,0:T(8,128)S(1)}, u32[]{:S(2)}, u32[]{:S(2)}) collective-permute-start(f32[31,8,128]{2,1,0:T(8,128)S(1)} %get-tuple-element.14), channel_id=1, source_target_pairs={{4,8},{8,4},{12,16},{16,12},{20,24},{24,20},{5,9},{9,5},{13,17},{1... | collective-permute-start | bytes 380936 | tf_op jit(solution)/shard_map/ppermute | solution.py:514
  11.3 0.1 collective-permute-start.5
  11.4 0.0 collective-permute-done.col_far
  11.4 0.0 collective-permute-done.1.col_near
  11.4 0.1 pack_corners.1
  11.5 3.6 %collective-permute-start.2 = (f32[7,8,128]{2,1,0:T(8,128)S(1)}, f32[7,8,128]{2,1,0:T(8,128)S(1)}, u32[]{:S(2)}, u32[]{:S(2)}) collective-permute-start(f32[7,8,128]{2,1,0:T(8,128)S(1)} %get-tuple-element.12), channel_id=1, source_target_pairs={{4,8},{8,4},{12,16},{16,12},{20,24},{24,20},{5,9},{9,5},{13,17},{1... | collective-permute-start | bytes 86024 | tf_op jit(solution)/shard_map/ppermute | solution.py:514
  15.0 0.1 collective-permute-start.3
  15.1 1.5 %collective-permute-done.2.corner_far = f32[7,8,128]{2,1,0:T(8,128)S(1)} collective-permute-done((f32[7,8,128]{2,1,0:T(8,128)S(1)}, f32[7,8,128]{2,1,0:T(8,128)S(1)}, u32[]{:S(2)}, u32[]{:S(2)}) %collective-permute-start.2) | collective-permute-done | bytes 28704 | tf_op jit(solution)/shard_map/ppermute | solution.py:514
  16.7 0.0 collective-permute-done.3.corner_near
  16.7 0.0 collective-permute-done.4.row_far
  16.7 0.0 collective-permute-done.5.row_near
  16.7 3.1 %model.1 = (f32[4,16,128]{2,1,0:T(8,128)}, f32[4,16,128]{2,1,0:T(8,128)}, f32[3,16,128]{2,1,0:T(8,128)}) custom-call(f32[7,8,128]{2,1,0:T(8,128)S(1)} %collective-permute-done.col_far, f32[7,8,128]{2,1,0:T(8,128)S(1)} %collective-permute-done.1.col_near, f32[7,8,128]{2,1,0:T(8,128)S(1)} %collective-permute-done.2.corner_far, ...), custom_call_target="tpu_custom_call" | custom-call | tf_op jit(solution)/shard_map/model/pallas_call | solution.py:558
Async XLA Ops:
  1.7 9.6 %collective-permute-start = (f32[7,8,128]{2,1,0:T(8,128)S(1)}, f32[7,8,128]{2,1,0:T(8,128)S(1)}, u32[]{:S(2)}, u32[]{:S(2)}) collective-permute-start(f32[7,8,128]{2,1,0:T(8,128)S(1)} %get-tuple-element.10), channel_id=1, source_target_pairs={{1,2},{2,1},{5,6},{6,5},{9,10},{10,9},{13,14},{14,13},{17,18},{18,... | collective-permute-start | bytes 86024 | tf_op jit(solution)/shard_map/ppermute | solution.py:514
  2.4 9.0 %collective-permute-start.1 = (f32[7,8,128]{2,1,0:T(8,128)S(1)}, f32[7,8,128]{2,1,0:T(8,128)S(1)}, u32[]{:S(2)}, u32[]{:S(2)}) collective-permute-start(f32[7,8,128]{2,1,0:T(8,128)S(1)} %get-tuple-element.11), channel_id=1, source_target_pairs={{0,1},{1,0},{2,3},{3,2},{4,5},{5,4},{6,7},{7,6},{8,9},{9,8},{10,11... | collective-permute-start | bytes 86024 | tf_op jit(solution)/shard_map/ppermute | solution.py:514
  7.0 9.7 %collective-permute-start.4 = (f32[31,8,128]{2,1,0:T(8,128)S(1)}, f32[31,8,128]{2,1,0:T(8,128)S(1)}, u32[]{:S(2)}, u32[]{:S(2)}) collective-permute-start(f32[31,8,128]{2,1,0:T(8,128)S(1)} %get-tuple-element.14), channel_id=1, source_target_pairs={{4,8},{8,4},{12,16},{16,12},{20,24},{24,20},{5,9},{9,5},{13,17},{1... | collective-permute-start | bytes 380936 | tf_op jit(solution)/shard_map/ppermute | solution.py:514
  11.3 5.4 %collective-permute-start.5 = (f32[31,8,128]{2,1,0:T(8,128)S(1)}, f32[31,8,128]{2,1,0:T(8,128)S(1)}, u32[]{:S(2)}, u32[]{:S(2)}) collective-permute-start(f32[31,8,128]{2,1,0:T(8,128)S(1)} %get-tuple-element.15), channel_id=1, source_target_pairs={{0,4},{4,0},{8,12},{12,8},{16,20},{20,16},{24,28},{28,24},{1,5},{5... | collective-permute-start | bytes 380936 | tf_op jit(solution)/shard_map/ppermute | solution.py:514
  11.5 5.2 %collective-permute-start.2 = (f32[7,8,128]{2,1,0:T(8,128)S(1)}, f32[7,8,128]{2,1,0:T(8,128)S(1)}, u32[]{:S(2)}, u32[]{:S(2)}) collective-permute-start(f32[7,8,128]{2,1,0:T(8,128)S(1)} %get-tuple-element.12), channel_id=1, source_target_pairs={{4,8},{8,4},{12,16},{16,12},{20,24},{24,20},{5,9},{9,5},{13,17},{1... | collective-permute-start | bytes 86024 | tf_op jit(solution)/shard_map/ppermute | solution.py:514
  15.0 1.6 %collective-permute-start.3 = (f32[7,8,128]{2,1,0:T(8,128)S(1)}, f32[7,8,128]{2,1,0:T(8,128)S(1)}, u32[]{:S(2)}, u32[]{:S(2)}) collective-permute-start(f32[7,8,128]{2,1,0:T(8,128)S(1)} %get-tuple-element.13), channel_id=1, source_target_pairs={{0,4},{4,0},{8,12},{12,8},{16,20},{20,16},{24,28},{28,24},{1,5},{5... | collective-permute-start | bytes 86024 | tf_op jit(solution)/shard_map/ppermute | solution.py:514
